TPU v7x, 512 devices: a whole 4x8x8 slice. The times are simulated.
512 devices in a mesh: ctx: 16 (over y, x_hi), cand: 8 (over z), head: 4 (over x_lo, core).
Axes of the slice: x: 4 (x_hi: 2, x_lo: 2; x = x_hi * 2 + x_lo), y: 8, z: 8, core: 2. Of those that a mesh axis runs over, the one named last changes fastest.
Arguments:
- query: bfloat16 [8, 256, 8192], P('cand', ('ctx', 'head')), may hold values from -12 to 12
- prefix_keys: bfloat16 [32768, 1024], P(('ctx', 'cand'), 'head'), may hold values from -12 to 12
- prefix_value_cache: bfloat16 [32768, 1024], P(('ctx', 'cand'), 'head'), may hold values from -6 to 6
- cont_keys: bfloat16 [8, 256, 1024], P('cand', ('ctx', 'head')), may hold values from -12 to 12
- continuation_values: bfloat16 [8, 256, 1024], P('cand', ('ctx', 'head')), may hold values from -6 to 6
- cont_lengths: int32 [8, 8], P('cand'), may hold values from 1 to 128, 256 in all within a row
Outputs:
- attended: bfloat16 [8, 256, 8192], P('cand', ('ctx', 'head'))
Inputs may be any that keep to these rules, and one draw needn't show every extreme that they name: `cont_lengths`: each row sums to 256; its largest entry is 128.
All inputs are finite; a program needn't handle non-finite values.
Results may differ from a plain program's by a relative error of at most 0.0055.
Values may be sent and summed in bfloat16 or wider, within the bound.
A program may use at most 64 MiB of HBM per device.

v0:
```python
import jax
import jax.numpy as jnp
from jax import lax
from jax.sharding import PartitionSpec as P

QUERY_HEADS = 64
KEY_VALUE_HEADS = 8
HEAD_SIZE = 128


NEG_FILL = -1e30


def split_heads(flat, kv_heads):
    lead = flat.shape[0]
    shaped = flat.reshape(lead, kv_heads, -1, HEAD_SIZE)
    return jnp.transpose(shaped, (1, 0, 2, 3)).reshape(kv_heads, -1, HEAD_SIZE)


def empty_state(kv_heads, query_rows):
    return (
        jnp.full((kv_heads, query_rows), NEG_FILL, jnp.float32),
        jnp.zeros((kv_heads, query_rows), jnp.float32),
        jnp.zeros((kv_heads, query_rows, HEAD_SIZE), jnp.float32),
    )


def attend(state, q_heads, k_heads, v_heads, allowed):
    running_max, running_sum, weighted = state
    scores = jnp.einsum(
        "hrd,hkd->hrk", q_heads, k_heads, preferred_element_type=jnp.float32
    ) * HEAD_SIZE ** (-0.5)
    if allowed is not None:
        scores = jnp.where(allowed, scores, NEG_FILL)
    new_max = jnp.maximum(running_max, jnp.max(scores, axis=-1))
    weights = jnp.exp(scores - new_max[..., None])
    if allowed is not None:
        weights = jnp.where(allowed, weights, 0.0)
    fading = jnp.exp(running_max - new_max)
    running_sum = fading * running_sum + jnp.sum(weights, axis=-1)
    weighted = fading[..., None] * weighted + jnp.einsum(
        "hrk,hkd->hrd", weights.astype(jnp.bfloat16), v_heads, preferred_element_type=jnp.float32
    )
    return (new_max, running_sum, weighted)


def prefix_pass(state, q_heads, k_heads, v_heads):
    key_rows = k_heads.shape[1]
    block_rows = 512
    blocks = key_rows // block_rows
    kv_heads = k_heads.shape[0]
    keys_blocked = jnp.transpose(
        k_heads.reshape(kv_heads, blocks, block_rows, HEAD_SIZE), (1, 0, 2, 3)
    )
    values_blocked = jnp.transpose(
        v_heads.reshape(kv_heads, blocks, block_rows, HEAD_SIZE), (1, 0, 2, 3)
    )

    def scan_block(carry, pair):
        return (attend(carry, q_heads, pair[0], pair[1], None), None)

    result, unused = lax.scan(scan_block, state, (keys_blocked, values_blocked))
    return result


def to_tokens(state, token_rows):
    running_max, running_sum, weighted = state
    kv_heads = running_max.shape[0]
    top_t = jnp.transpose(running_max.reshape(kv_heads, token_rows, -1), (1, 0, 2)).reshape(
        token_rows, -1
    )
    sum_t = jnp.transpose(running_sum.reshape(kv_heads, token_rows, -1), (1, 0, 2)).reshape(
        token_rows, -1
    )
    weighted_t = jnp.transpose(
        weighted.reshape(kv_heads, token_rows, -1, HEAD_SIZE), (1, 0, 2, 3)
    ).reshape(token_rows, -1)
    return (top_t, sum_t, weighted_t)


def join(first, second):
    new_max = jnp.maximum(first[0], second[0])
    fade_one = jnp.exp(first[0] - new_max)
    fade_two = jnp.exp(second[0] - new_max)
    token_rows, heads_count = new_max.shape
    running_sum = fade_one * first[1] + fade_two * second[1]
    weighted = (
        first[2].reshape(token_rows, heads_count, HEAD_SIZE) * fade_one[..., None]
        + second[2].reshape(token_rows, heads_count, HEAD_SIZE) * fade_two[..., None]
    )
    return (new_max, running_sum, weighted.reshape(token_rows, -1))


def per_device(
    query, prefix_keys, prefix_value_cache, cont_keys, continuation_values, cont_lengths
):
    kv_heads = prefix_keys.shape[1] // HEAD_SIZE
    heads_per_group = QUERY_HEADS // KEY_VALUE_HEADS
    own_query, own_keys, own_values = (
        lax.all_to_all(query[0], "head", split_axis=1, concat_axis=0, tiled=True),
        lax.all_to_all(cont_keys[0], "head", split_axis=1, concat_axis=0, tiled=True),
        lax.all_to_all(continuation_values[0], "head", split_axis=1, concat_axis=0, tiled=True),
    )
    own_rows = own_query.shape[0]
    ctx_count = lax.axis_size("ctx")
    group_rows = own_rows * ctx_count
    ends = jnp.cumsum(cont_lengths[0])

    def segment_of(positions):
        return jnp.sum((ends[None, :] <= positions[:, None]).astype(jnp.int32), axis=1)

    own_pos = lax.axis_index("ctx") * own_rows + jnp.arange(own_rows, dtype=jnp.int32)
    own_segment = segment_of(own_pos)
    own_heads = split_heads(own_query, kv_heads)
    pieces = (
        lax.all_gather(own_keys, "ctx", axis=0, tiled=True),
        lax.all_gather(own_values, "ctx", axis=0, tiled=True),
    )
    piece_rows = pieces[0].shape[0]
    positions = jnp.arange(piece_rows, dtype=jnp.int32)
    allowed = (own_segment[:, None] == segment_of(positions)[None, :]) & (
        positions[None, :] <= own_pos[:, None]
    )
    allowed = jnp.repeat(allowed, heads_per_group, axis=0)[None]
    recent = attend(
        empty_state(kv_heads, own_rows * heads_per_group),
        own_heads,
        split_heads(pieces[0], kv_heads),
        split_heads(pieces[1], kv_heads),
        allowed,
    )
    all_query = lax.all_gather(own_query, "ctx", axis=0, tiled=True)
    all_heads = split_heads(all_query, kv_heads)
    pieces = (
        lax.all_gather(prefix_keys, "cand", axis=0, tiled=True),
        lax.all_gather(prefix_value_cache, "cand", axis=0, tiled=True),
    )
    state = prefix_pass(
        empty_state(kv_heads, group_rows * heads_per_group),
        all_heads,
        split_heads(pieces[0], kv_heads),
        split_heads(pieces[1], kv_heads),
    )
    top_t, sum_t, weighted_t = to_tokens(state, group_rows)
    received = (
        lax.all_to_all(weighted_t, "ctx", split_axis=0, concat_axis=0, tiled=True),
        lax.all_to_all(top_t, "ctx", split_axis=0, concat_axis=0, tiled=True),
        lax.all_to_all(sum_t, "ctx", split_axis=0, concat_axis=0, tiled=True),
    )
    heads_count = top_t.shape[1]
    weighted_s = received[0].reshape(ctx_count, own_rows, heads_count, HEAD_SIZE)
    top_s = received[1].reshape(ctx_count, own_rows, heads_count)
    sum_s = received[2].reshape(ctx_count, own_rows, heads_count)
    best = jnp.max(top_s, axis=0)
    fading = jnp.exp(top_s - best[None])
    cached = (
        best,
        jnp.sum(fading * sum_s, axis=0),
        jnp.sum(fading[..., None] * weighted_s, axis=0).reshape(own_rows, -1),
    )
    final = join(cached, to_tokens(recent, own_rows))
    heads_count = final[0].shape[1]
    output = (
        (final[2].reshape(own_rows, heads_count, HEAD_SIZE) / final[1][..., None])
        .reshape(own_rows, -1)
        .astype(jnp.bfloat16)
    )
    returned = lax.all_to_all(output, "head", split_axis=0, concat_axis=1, tiled=True)
    return returned[None]


def solution(mesh):
    return jax.shard_map(
        per_device,
        mesh=mesh,
        in_specs=(
            P("cand", ("ctx", "head"), None),
            P(("ctx", "cand"), "head"),
            P(("ctx", "cand"), "head"),
            P("cand", ("ctx", "head"), None),
            P("cand", ("ctx", "head"), None),
            P("cand", None),
        ),
        out_specs=P("cand", ("ctx", "head"), None),
        check_vma=False,
    )
```

profile of v0, /device:TPU:1, one launch (start us, length us, event | category | flops | bytes accessed | tf_op | source)
XLA Modules:
  0.0 400.4 jit_solution(10681114816348384850)
XLA Ops:
  6.5 1.6 copy.87
  8.3 1.7 copy.92
  10.0 13.4 %all_to_all.97 = bf16[4,4,2048]{2,0,1:T(4,128)(2,1)S(1)} all-to-all(bf16[4,4,2048]{2,0,1:T(4,128)(2,1)} %bitcast.151), channel_id=1, replica_groups=mesh['ctx'=16,'cand'=8,'head'=4] {'head'}, dimensions={1} | all-to-all | bytes 131072 | tf_op jit(solution)/shard_map/all_to_all | solution.py:100
  23.4 0.6 all_to_all.73
  24.1 4.1 %all-to-all-start.3 = ((bf16[4,4,256]{2,0,1:T(4,128)(2,1)}), bf16[4,4,256]{2,0,1:T(4,128)(2,1)S(1)}, u32[]{:S(2)}, u32[]{:S(2)}) async-start(bf16[4,4,256]{2,0,1:T(4,128)(2,1)} %bitcast.154), calls=%async_computation.3 | async-start | bytes 16384 | tf_op jit(solution)/shard_map/all_to_all | solution.py:101
  28.2 25.4 %all-gather.4.cloned.1.call-done = bf16[2048,256]{0,1:T(8,128)(2,1)} async-done(((bf16[256,256]{0,1:T(8,128)(2,1)}), bf16[2048,256]{0,1:T(8,128)(2,1)}) %all-gather.4.cloned.1.call-update) | async-done | bytes 1048592 | tf_op jit(solution)/shard_map/all_gather | solution.py:135
  53.6 2.3 copy.88
  55.9 41.4 %all-gather.8.cloned.1.call-done = bf16[2048,256]{0,1:T(8,128)(2,1)} async-done(((bf16[256,256]{0,1:T(8,128)(2,1)}), bf16[2048,256]{0,1:T(8,128)(2,1)}) %all-gather.8.cloned.1.call-update) | async-done | bytes 1048592 | tf_op jit(solution)/shard_map/all_gather | solution.py:136
  97.3 2.3 copy.93
  99.5 84.2 %all-gather.6.cloned.1.call-done = bf16[256,2048]{1,0:T(8,128)(2,1)} async-done(((bf16[16,2048]{1,0:T(8,128)(2,1)}), bf16[256,2048]{1,0:T(8,128)(2,1)}) %all-gather.6.cloned.1.call-update) | async-done | bytes 1048592 | tf_op jit(solution)/shard_map/all_gather | solution.py:132
  183.7 2.3 copy.90
  186.0 1.7 copy.91
  187.7 7.8 %all-to-all-start.4 = ((bf16[4,4,256]{2,0,1:T(4,128)(2,1)}), bf16[4,4,256]{2,0,1:T(4,128)(2,1)S(1)}, u32[]{:S(2)}, u32[]{:S(2)}) async-start(bf16[4,4,256]{2,0,1:T(4,128)(2,1)} %bitcast.28), calls=%async_computation.4 | async-start | bytes 16384 | tf_op jit(solution)/shard_map/all_to_all | solution.py:102
  195.5 29.6 %while.15 = (s32[]{:T(128)}, f32[2,2048]{1,0:T(2,128)S(1)}, f32[2,2048]{1,0:T(2,128)S(1)}, f32[2,2048,128]{2,1,0:T(8,128)S(1)}, bf16[4,2,512,128]{3,2,0,1:T(8,12...) while((s32[]{:T(128)}, f32[2,2048]{1,0:T(2,128)S(1)}, ...), condition=%wide.region_3.4_spmd.clone, body=%wide.region_0.3_spmd.clone.sunk | while | flops 1092112384 | bytes 31195256 | solution.py:62
  195.5 2.2 bitcast_reduce_fusion.3
  197.7 1.4 fusion.55
  199.2 3.7 fusion.57
  202.9 2.2 bitcast_reduce_fusion.3
  205.1 1.4 fusion.55
  206.6 3.7 fusion.57
  210.3 2.2 bitcast_reduce_fusion.3
  212.5 1.4 fusion.55
  214.0 3.7 fusion.57
  217.7 2.2 bitcast_reduce_fusion.3
  219.9 1.4 fusion.55
  221.4 3.7 fusion.57
  225.1 0.2 reshape.189
  225.2 0.1 copy.96
  225.3 0.1 all_to_all.74
  225.5 0.7 reshape.203
  226.2 4.0 all-to-all-start.1
  230.2 0.2 reshape.201
  230.4 0.1 copy.111
  230.5 0.1 all_to_all.86
  230.7 0.7 reshape.205
  231.4 7.8 %all-to-all-done.1 = f32[16,1,256]{2,1,0:T(1,128)S(1)} async-done(((f32[16,1,256]{2,1,0:T(1,128)}), f32[16,1,256]{2,1,0:T(1,128)S(1)}, u32[]{:S(2)}, u32[]{:S(2)}) %all-to-all-start.1) | async-done | bytes 16416 | tf_op jit(solution)/shard_map/all_to_all | solution.py:147
  239.1 3.5 all-to-all-start.5
  242.6 1.5 copy_bitcast_fusion
  244.1 2.7 all_to_all.76
  246.8 4.6 %all-to-all-done.5 = f32[16,1,256]{2,1,0:T(1,128)S(1)} async-done(((f32[16,1,256]{2,1,0:T(1,128)}), f32[16,1,256]{2,1,0:T(1,128)S(1)}, u32[]{:S(2)}, u32[]{:S(2)}) %all-to-all-start.5) | async-done | bytes 16416 | tf_op jit(solution)/shard_map/all_to_all | solution.py:148
  251.5 4.5 %all-to-all-start.2 = ((f32[16,16,2048]{2,1,0:T(8,128)}), f32[16,16,2048]{2,1,0:T(8,128)S(1)}, u32[]{:S(2)}, u32[]{:S(2)}) async-start(f32[16,16,2048]{2,1,0:T(8,128)} %all_to_all.76), calls=%async_computation.2 | async-start | bytes 4194304 | tf_op jit(solution)/shard_map/all_to_all | solution.py:146
  256.0 0.2 reduce-window.8
  256.5 73.7 %all_gather.19 = bf16[256,256]{1,0:T(8,128)(2,1)S(1)} all-gather(bf16[16,256]{1,0:T(8,128)(2,1)S(1)} %all_to_all.85), channel_id=1, replica_groups=mesh['ctx'=16,'cand'=8,'head'=4] {'ctx'}, dimensions={0}, use_global_device_ids=true | all-gather | bytes 139264 | tf_op jit(solution)/shard_map/all_gather | solution.py:117
  330.1 0.1 copy.107
  330.2 0.1 copy.108
  330.3 29.3 %all_gather.18 = bf16[256,256]{1,0:T(8,128)(2,1)S(1)} all-gather(bf16[16,256]{1,0:T(8,128)(2,1)S(1)} %all_to_all.81), channel_id=1, replica_groups=mesh['ctx'=16,'cand'=8,'head'=4] {'ctx'}, dimensions={0}, use_global_device_ids=true | all-gather | bytes 139264 | tf_op jit(solution)/shard_map/all_gather | solution.py:116
  359.6 0.1 copy.102
  359.7 0.1 copy.103
  359.9 0.3 fusion.40
  360.3 0.2 fusion.21
  360.7 0.2 fusion.22
  361.0 0.5 broadcast.74
  361.5 0.7 reduce.2
  362.2 0.1 reshape.204
  362.3 0.7 reduce.3
  363.0 0.1 reshape.206
  363.4 0.1 mul.102
  363.6 0.1 mul.97
  363.7 0.1 div.12
  364.0 1.9 mul.91
  365.9 2.7 mul.92
  368.6 1.8 multiply_reduce_fusion
  370.6 22.7 %all_to_all.98 = bf16[4,4,2048]{2,1,0:T(4,128)(2,1)S(1)} all-to-all(bf16[4,4,2048]{2,1,0:T(4,128)(2,1)S(1)} %fusion.30), channel_id=1, replica_groups=mesh['ctx'=16,'cand'=8,'head'=4] {'head'}, dimensions={0} | all-to-all | bytes 131072 | tf_op jit(solution)/shard_map/all_to_all | solution.py:168
  393.2 0.6 copy.144
  (56 shorter events, 1.9 us)
Async XLA Ops:
  6.5 47.0 %all-gather.4.cloned.1.call-start = ((), (), s32[]{:S(2)}) async-start(), calls=%async_computation.7 | async-start | bytes 1179648 | tf_op jit(solution)/shard_map/all_gather | solution.py:135
  8.2 89.0 %all-gather.8.cloned.1.call-start = ((), (), s32[]{:S(2)}) async-start(), calls=%async_computation.9 | async-start | bytes 1179648 | tf_op jit(solution)/shard_map/all_gather | solution.py:136
  9.9 173.8 %all-gather.6.cloned.1.call-start = ((), (), s32[]{:S(2)}) async-start(), calls=%async_computation.8 | async-start | bytes 1114112 | tf_op jit(solution)/shard_map/all_gather | solution.py:132
  24.1 163.7 %all-to-all-start.3 = ((bf16[4,4,256]{2,0,1:T(4,128)(2,1)}), bf16[4,4,256]{2,0,1:T(4,128)(2,1)S(1)}, u32[]{:S(2)}, u32[]{:S(2)}) async-start(bf16[4,4,256]{2,0,1:T(4,128)(2,1)} %bitcast.154), calls=%async_computation.3 | async-start | bytes 16384 | tf_op jit(solution)/shard_map/all_to_all | solution.py:101
  187.7 38.5 %all-to-all-start.4 = ((bf16[4,4,256]{2,0,1:T(4,128)(2,1)}), bf16[4,4,256]{2,0,1:T(4,128)(2,1)S(1)}, u32[]{:S(2)}, u32[]{:S(2)}) async-start(bf16[4,4,256]{2,0,1:T(4,128)(2,1)} %bitcast.28), calls=%async_computation.4 | async-start | bytes 16384 | tf_op jit(solution)/shard_map/all_to_all | solution.py:102
  226.2 12.9 %all-to-all-start.1 = ((f32[16,1,256]{2,1,0:T(1,128)}), f32[16,1,256]{2,1,0:T(1,128)S(1)}, u32[]{:S(2)}, u32[]{:S(2)}) async-start(f32[16,1,256]{2,1,0:T(1,128)} %reshape.203), calls=%async_computation.1 | async-start | bytes 32768 | tf_op jit(solution)/shard_map/all_to_all | solution.py:147
  239.1 12.3 %all-to-all-start.5 = ((f32[16,1,256]{2,1,0:T(1,128)}), f32[16,1,256]{2,1,0:T(1,128)S(1)}, u32[]{:S(2)}, u32[]{:S(2)}) async-start(f32[16,1,256]{2,1,0:T(1,128)} %reshape.205), calls=%async_computation.5 | async-start | bytes 32768 | tf_op jit(solution)/shard_map/all_to_all | solution.py:148
  246.8 9.1 %copy-start = (s32[1,8]{1,0:T(1,128)S(1)}, s32[1,8]{1,0:T(1,128)}, u32[]{:S(2)}) copy-start(s32[1,8]{1,0:T(1,128)} %param.13) | copy-start | bytes 100
  251.5 117.2 %all-to-all-start.2 = ((f32[16,16,2048]{2,1,0:T(8,128)}), f32[16,16,2048]{2,1,0:T(8,128)S(1)}, u32[]{:S(2)}, u32[]{:S(2)}) async-start(f32[16,16,2048]{2,1,0:T(8,128)} %all_to_all.76), calls=%async_computation.2 | async-start | bytes 4194304 | tf_op jit(solution)/shard_map/all_to_all | solution.py:146
Sparse Core Ops, SparseCore 0:
  9.4 44.1 all-gather.3
  55.6 41.6 all-gather.7
  100.4 83.2 all-gather.5
where the time goes:
time: 401 us; the launch traced here: 400 us
  waiting for transfers between devices  163 us (41%)
  blocking collectives  139 us (35%)
  local copies, waits for them, and re-layouts  26.5 us (7%)
  matrix products  24.1 us (6%)
  starting transfers between devices  23.9 us (6%)
  between operations  13.4 us (3%)
  other arithmetic  9.81 us (2%)
    all_gather x1, waiting for transfers between devices, per_device(): all_query = lax.all_gather(own_query, 'ctx', axis=0, tiled=True)  84.2 us
    all_gather x1, blocking collectives, per_device(): lax.all_gather(own_values, 'ctx', axis=0, tiled=True)  73.7 us
    all_gather x1, waiting for transfers between devices, per_device(): lax.all_gather(prefix_value_cache, 'cand', axis=0, tiled=True)  41.4 us
    all_gather x1, blocking collectives, per_device(): lax.all_gather(own_keys, 'ctx', axis=0, tiled=True)  29.3 us
    all_gather x1, waiting for transfers between devices, per_device(): lax.all_gather(prefix_keys, 'cand', axis=0, tiled=True)  25.4 us
    all_to_all x1, blocking collectives, per_device(): lax.all_to_all(output, 'head', split_axis=0, concat_axis=1, tiled=True)  22.7 us
    dot_general x5, matrix products, attend(): jnp.einsum('hrk,hkd->hrd', weights.astype(jnp.bfloat16), v_heads, preferr...  14.9 us
    all_to_all x1, blocking collectives, per_device(): lax.all_to_all(query[0], 'head', split_axis=1, concat_axis=0, tiled=True)  13.4 us
  transfers between devices with their start and end apart: 8, of which 5 were waited for; matrix products, arithmetic and copies ran while one was open for 13% of the time, Pallas kernels for 0%

commit v1 on v0

v1 whole, which is shorter than its diff:
```python
import functools
import math

import jax
import jax.numpy as jnp
from jax import lax
from jax.experimental import pallas as pl
from jax.experimental.pallas import tpu as pltpu
from jax.sharding import PartitionSpec as P

MESH = pl.DeviceIdType.MESH
BF = jnp.bfloat16
F32 = jnp.float32
HEAD_SIZE = 128
SCALE = HEAD_SIZE ** -0.5
EXP2_SCALE = SCALE * math.log2(math.e)
TILE = 256
CHUNK = TILE + 64
MASKED = -1e30


def dot_nt(a, b):
    return lax.dot_general(a, b, (((1,), (1,)), ((), ())), preferred_element_type=F32)


def lanes(parts):
    return [p[:, i : i + 128] for p in parts for i in range(0, p.shape[1], 128)]


def fold(op, parts):
    parts = list(parts)
    while len(parts) > 1:
        pairs = [op(a, b) for a, b in zip(parts[::2], parts[1::2])]
        parts = pairs + (parts[-1:] if len(parts) % 2 else [])
    return parts[0]


def advance(state, scores, values):
    top = jnp.max(fold(jnp.maximum, lanes(scores)), axis=1, keepdims=True)
    if state is None:
        top = jnp.broadcast_to(top, (top.shape[0], 128))
    else:
        old = state[0]
        top = jnp.maximum(old, top)
        fade = jnp.exp2((old - top) * EXP2_SCALE)
    weights = [
        [jnp.exp2((s - top) * EXP2_SCALE) for s in lanes([part])] for part in scores
    ]
    total = fold(jnp.add, [w for part in weights for w in part])
    mixed = fold(
        jnp.add,
        [
            jnp.dot(jnp.concatenate([w.astype(BF) for w in part], axis=1), v, preferred_element_type=F32)
            for part, v in zip(weights, values)
        ],
    )
    if state is not None:
        total = total + fade * state[1]
        mixed = mixed + fade * state[2]
    return top, total, mixed


def right_slot(s):
    return 2 * s - 1 if s else 0


def left_slot(n, s):
    return 2 * s if s < n // 2 else n - 1


def kernel(
    n, q_ref, ck_ref, cv_ref, len_ref, pk_ref, pv_ref, out_ref,
    stage, outbox, inbox, kvb, qb, top, total, mixed, ckb, cvb,
    osend, lsend, orecv, lrecv, fsend, frecv,
    own_sem, box_send, box_recv, pair_send, pair_recv, kv_send, kv_recv,
    q_send, q_recv, o_send, o_recv, l_send, l_recv, f_send, f_recv,
):
    half = n // 2
    ctx, z, head = lax.axis_index("ctx"), lax.axis_index("cand"), lax.axis_index("head")
    y, xh, core = ctx // 2, ctx % 2, head % 2
    me = xh * 4 + head
    kv_head = 2 * head + xh
    u = z + core * (y - z)
    v = y + core * (z - y)

    def device(uu, vv):
        return ((vv + core * (uu - vv)) * 2 + xh, uu + core * (vv - uu), head)

    def around(a, s):
        return lax.rem(a + s + n, n)

    members = [(e // 4, e % 4) for e in range(8)]
    here = (core == 0) | (y == z)

    def source(e):
        return (v * 2 + members[e][0], u, members[e][1])

    def target(e):
        return (y * 2 + members[e][0], z, members[e][1]) if e % 2 == 0 else (z * 2 + members[e][0], y, members[e][1])

    def other(e):
        return jnp.logical_not((me == e) & here)

    barrier = pltpu.get_barrier_semaphore()

    def greet(to):
        pl.semaphore_signal(barrier, inc=1, device_id=to, device_id_type=MESH)

    for e in range(8):
        @pl.when(other(e))
        def _():
            greet(source(e))
            greet(target(e))
    partner = (y * 2 + 1 - xh, z, head)
    greet(partner)
    for s in range(1, n):
        greet(device(u, around(v, s)))
    right, left = device(around(u, 1), v), device(around(u, -1), v)
    greet(right)
    greet(left)

    own_copies = [
        pltpu.make_async_copy(
            ref.at[:, pl.ds(pl.multiple_of(xh * 128, 128), 128)], kvb.at[0, 0, i], own_sem.at[i]
        )
        for i, ref in enumerate((pk_ref, pv_ref))
    ]
    for c in own_copies:
        c.start()

    ends, so_far = [], 0
    for c in range(8):
        so_far = so_far + len_ref[0, c]
        ends.append(so_far)
    place = lax.broadcasted_iota(jnp.int32, (8, 128), 1) + 128 * lax.broadcasted_iota(jnp.int32, (8, 128), 0)
    segment = fold(jnp.add, [jnp.where(end <= place, 1.0, 0.0) for end in ends])
    for k in range(8):
        for j in range(8):
            stage[k, j * 4 : j * 4 + 4, :] = q_ref[0, :, (k * 8 + j) * 128 : (k * 8 + j + 1) * 128].astype(F32)
        stage[k, 32:36, :] = ck_ref[0, :, k * 128 : k * 128 + 128].astype(F32)
        stage[k, 36:40, :] = cv_ref[0, :, k * 128 : k * 128 + 128].astype(F32)
        stage[k, 40:48, :] = segment
        outbox[k] = stage[k].astype(BF)

    pl.semaphore_wait(barrier, 1 + (n - 1) + 2 + 16 - 2 * here.astype(jnp.int32))

    def remote(src, dst, send, recv, to):
        return pltpu.make_async_remote_copy(
            src_ref=src, dst_ref=dst, send_sem=send, recv_sem=recv, device_id=to, device_id_type=MESH
        )

    pair = [
        remote(
            ref.at[:, pl.ds(pl.multiple_of((1 - xh) * 128, 128), 128)],
            kvb.at[0, 1, i], pair_send.at[i], pair_recv.at[i], partner,
        )
        for i, ref in enumerate((pk_ref, pv_ref))
    ]
    for c in pair:
        c.start()

    def box(e):
        k = 2 * members[e][1] + members[e][0]
        return remote(outbox.at[k], inbox.at[me], box_send.at[e], box_recv.at[me], target(e))

    def box_in(e):
        return remote(outbox.at[0], inbox.at[e], box_send.at[e], box_recv.at[e], source(e))

    for e in range(8):
        @pl.when(other(e))
        def _():
            box(e).start()

        @pl.when(jnp.logical_not(other(e)))
        def _():
            inbox[e] = outbox[kv_head]

    def kv_copies(s, sub):
        rs, ls = right_slot(s), left_slot(n, s)
        out = []
        if s < half or sub == 0:
            out.append(remote(kvb.at[right_slot(s - 1), sub], kvb.at[rs, sub], kv_send.at[rs, sub], kv_recv.at[rs, sub], right))
        if s < half or sub == 1:
            out.append(remote(kvb.at[left_slot(n, s - 1) if s > 1 else 0, sub], kvb.at[ls, sub], kv_send.at[ls, sub], kv_recv.at[ls, sub], left))
        return out

    def kv_begin(s, sub):
        if s <= half:
            for c in kv_copies(s, sub):
                c.start()

    def kv_arrive(s, sub):
        if s <= half:
            if s == half:
                for c in kv_copies(s, sub):
                    c.wait_recv()
                return
            copies, nexts = kv_copies(s, sub), (kv_copies(s + 1, sub))
            copies[0].wait_recv()
            copies[1].wait_recv()
            for c in nexts:
                c.start()

    for c in own_copies:
        c.wait()
    kv_begin(1, 0)

    q_right, q_left = device(u, around(v, 1)), device(u, around(v, -1))

    def q_copies(s):
        rs, ls = right_slot(s), left_slot(n, s)
        first, second = (pl.ds(0, CHUNK), pl.ds(0, CHUNK)) if s < half else (pl.ds(0, CHUNK // 2), pl.ds(CHUNK // 2, CHUNK // 2))
        return [
            remote(qb.at[right_slot(s - 1), first], qb.at[rs, first], q_send.at[0, s - 1], q_recv.at[0, s - 1], q_right),
            remote(qb.at[left_slot(n, s - 1) if s > 1 else 0, second], qb.at[ls, second], q_send.at[1, s - 1], q_recv.at[1, s - 1], q_left),
        ]

    for e in range(8):
        @pl.when(other(e))
        def _():
            box_in(e).wait_recv()
    for e in range(8):
        qb[0, e * 32 : e * 32 + 32, :] = inbox[e, 0:32, :]
        extra = inbox[e, 32:48, :].astype(F32)
        stage[0, e * 4 : e * 4 + 4, :] = extra[0:4]
        stage[1, e * 4 : e * 4 + 4, :] = extra[4:8]
    qb[0, TILE : TILE + 32, :] = stage[0, 0:32, :].astype(BF)
    qb[0, TILE + 32 : TILE + 64, :] = stage[1, 0:32, :].astype(BF)
    for c in q_copies(1):
        c.start()
    for c in pair:
        c.wait_recv()
    kv_begin(1, 1)

    def store(r, state):
        top[r], total[r], mixed[r] = state

    def update(r, slots, first=False):
        q = qb[r, 0:TILE, :]
        pieces = [(s, ab) for s in slots for ab in (0, 1)]
        scores = [dot_nt(q, kvb[s, ab, 0]) for s, ab in pieces]
        values = [kvb[s, ab, 1] for s, ab in pieces]
        return advance(None if first else (top[r], total[r], mixed[r]), scores, values)

    def sweep(low, high, slots, first=False):
        def one(r, _):
            store(r, update(r, slots, first))
            return 0

        lax.fori_loop(low, high, one, 0)

    sweep(0, 1, (0,), True)
    for s in range(1, half + 1):
        kv_arrive((s + 1) // 2, (s + 1) % 2)
        copies = q_copies(s)
        for c in copies:
            c.wait_recv()
        if s < half:
            for c in q_copies(s + 1):
                c.start()
        sweep(2 * s - 1, min(2 * s + 1, n), (0,), True)
    arrived = [((s + 1) // 2, (s + 1) % 2) for s in range(1, half + 1)]
    waiting = [(s, sub) for s in range(1, half + 1) for sub in (0, 1) if (s, sub) not in arrived]

    def arrive_until(s, sub):
        while waiting and waiting[0] <= (s, sub):
            kv_arrive(*waiting.pop(0))

    for r in range(n):
        d = -((r + 1) // 2) if r % 2 or r == n - 1 else r // 2
        at = pl.ds(pl.multiple_of(around(v, d) * 32, 32), 32)
        ckb[at, :] = qb[r, TILE : TILE + 32, :]
        cvb[at, :] = qb[r, TILE + 32 : TILE + 64, :]
    wide = min(128, 32 * n)
    marks = inbox[0, 32:48, :].astype(F32)
    row = lax.broadcasted_iota(jnp.int32, (TILE, wide), 0)
    slot = v * 32 + (row // 32) * 4 + row % 4
    lane = lax.broadcasted_iota(jnp.int32, (TILE, wide), 1)
    halves = range(32 * n // wide)
    own = fold(jnp.add, [
        jnp.sum(jnp.where(lane + h * wide == slot, marks[8 + h : 9 + h, :wide], 0.0), axis=1, keepdims=True) for h in halves
    ])
    scores = []
    for h in halves:
        allowed = (marks[8 + h : 9 + h, :wide] == own) & (lane + h * wide <= slot)
        scores.append(jnp.where(allowed, dot_nt(qb[0, 0:TILE, :], ckb[h * wide : (h + 1) * wide, :]), MASKED))
    store(0, advance((top[0], total[0], mixed[0]), scores, [cvb[h * wide : (h + 1) * wide, :] for h in halves]))

    for s in range(1, half):
        arrive_until(s, 1)
        slots = (right_slot(s), left_slot(n, s))
        sweep(0, n // 2, slots)
        arrive_until(s + 1, 0)
        sweep(n // 2, n, slots)
    arrive_until(half, 1)

    row = lax.broadcasted_iota(jnp.int32, (128, 128), 0)
    lane = lax.broadcasted_iota(jnp.int32, (128, 128), 1)
    diagonal = row == lane

    def finish(r):
        t, w, m = update(r, (n - 1,))
        w = jnp.sum(w, axis=1, keepdims=True)
        lse = t * SCALE + jnp.log(w)
        for h in range(2):
            lsend[r, h : h + 1, :] = jnp.sum(
                jnp.where(diagonal, lse[h * 128 : h * 128 + 128], 0.0), axis=0, keepdims=True
            )
        return m / w

    def o_copies(r, mirror, to):
        return [
            remote(osend.at[r], orecv.at[mirror], o_send.at[r], o_recv.at[mirror], to),
            remote(lsend.at[r], lrecv.at[mirror], l_send.at[r], l_recv.at[mirror], to),
        ]

    sent = []
    for r in range(n - 1, 0, -1):
        osend[r] = finish(r).astype(BF)
        if r == n - 1:
            copies = o_copies(r, r, device(u, around(v, half)))
        elif r % 2:
            copies = o_copies(r, r + 1, device(u, around(v, -((r + 1) // 2))))
        else:
            copies = o_copies(r, r - 1, device(u, around(v, r // 2)))
        for c in copies:
            c.start()
        sent += copies
    mine = finish(0)
    for c in sent:
        c.wait_recv()
    pieces = [lsend[0, 0:2, :]] + [lrecv[r, 0:2, :] for r in range(1, n)]
    largest = fold(jnp.maximum, pieces)
    shares = [jnp.exp(p - largest) for p in pieces]
    whole = fold(jnp.add, shares)
    shares = [p / whole for p in shares]
    for h in range(2):
        rows = slice(h * 128, h * 128 + 128)
        terms = []
        for r in range(n):
            share = jnp.sum(jnp.where(diagonal, shares[r][h : h + 1, :], 0.0), axis=1, keepdims=True)
            terms.append(share * (mine[rows] if r == 0 else orecv[r, rows, :].astype(F32)))
        fsend[rows, :] = fold(jnp.add, terms).astype(BF)

    def final(e):
        return remote(fsend.at[e * 32 : e * 32 + 32], frecv.at[kv_head], f_send.at[e], f_recv.at[kv_head], source(e))

    def final_in(e):
        k = 2 * members[e][1] + members[e][0]
        return remote(fsend.at[0:32], frecv.at[k], f_send.at[e], f_recv.at[k], target(e))

    for e in range(8):
        @pl.when(other(e))
        def _():
            final(e).start()

        @pl.when(jnp.logical_not(other(e)))
        def _():
            frecv[kv_head] = fsend[e * 32 : e * 32 + 32, :]

    for c in sent + pair + [c for s in range(1, half + 1) for sub in (0, 1) for c in kv_copies(s, sub)]:
        c.wait_send()
    for s in range(1, half + 1):
        for c in q_copies(s):
            c.wait_send()
    for e in range(8):
        @pl.when(other(e))
        def _():
            box(e).wait_send()
            final(e).wait_send()
            final_in(e).wait_recv()
    out_ref[...] = frecv[...]


def per_device(n, query, prefix_keys, prefix_value_cache, cont_keys, continuation_values, cont_lengths):
    rows = prefix_keys.shape[0]
    vmem = pl.BlockSpec(memory_space=pltpu.VMEM)
    anywhere = pl.BlockSpec(memory_space=pl.ANY)
    dma = pltpu.SemaphoreType.DMA
    out = pl.pallas_call(
        functools.partial(kernel, n),
        out_shape=jax.ShapeDtypeStruct((8, 32, 128), BF),
        in_specs=[vmem, vmem, vmem, pl.BlockSpec(memory_space=pltpu.SMEM), anywhere, anywhere],
        out_specs=vmem,
        scratch_shapes=[
            pltpu.VMEM((8, 48, 128), F32),
            pltpu.VMEM((8, 48, 128), BF),
            pltpu.VMEM((8, 48, 128), BF),
            pltpu.VMEM((n, 2, 2, rows, 128), BF),
            pltpu.VMEM((n, CHUNK, 128), BF),
            pltpu.VMEM((n, TILE, 128), F32),
            pltpu.VMEM((n, TILE, 128), F32),
            pltpu.VMEM((n, TILE, 128), F32),
            pltpu.VMEM((32 * n, 128), BF),
            pltpu.VMEM((32 * n, 128), BF),
            pltpu.VMEM((n, TILE, 128), BF),
            pltpu.VMEM((n, 8, 128), F32),
            pltpu.VMEM((n, TILE, 128), BF),
            pltpu.VMEM((n, 8, 128), F32),
            pltpu.VMEM((TILE, 128), BF),
            pltpu.VMEM((8, 32, 128), BF),
            dma((2,)), dma((8,)), dma((8,)), dma((2,)), dma((2,)), dma((n, 2)), dma((n, 2)),
            dma((2, n // 2)), dma((2, n // 2)), dma((n,)), dma((n,)), dma((n,)), dma((n,)), dma((8,)), dma((8,)),
        ],
        compiler_params=pltpu.CompilerParams(
            collective_id=0, has_side_effects=True, vmem_limit_bytes=48 * 1024 * 1024
        ),
        cost_estimate=pl.CostEstimate(flops=4_300_000_000, bytes_accessed=1_000_000, transcendentals=8_400_000),
    )(query, cont_keys, continuation_values, cont_lengths, prefix_keys, prefix_value_cache)
    return jnp.transpose(out.reshape(8, 8, 4, 128), (2, 0, 1, 3)).reshape(query.shape)


def solution(mesh):
    n = mesh.shape["cand"]
    return jax.shard_map(
        functools.partial(per_device, n),
        mesh=mesh,
        in_specs=(
            P("cand", ("ctx", "head"), None),
            P(("ctx", "cand"), "head"),
            P(("ctx", "cand"), "head"),
            P("cand", ("ctx", "head"), None),
            P("cand", ("ctx", "head"), None),
            P("cand", None),
        ),
        out_specs=P("cand", ("ctx", "head"), None),
        check_vma=False,
    )
```

time: 401 us -> 76.5 us (0.19)
  waiting for transfers between devices: 163 us -> 0 us
  blocking collectives: 139 us -> 0 us
  Pallas kernels: 0 us -> 69.7 us
  matrix products: 24.1 us -> 0 us
  starting transfers between devices: 23.9 us -> 0 us
  local copies, waits for them, and re-layouts: 26.5 us -> 5.33 us
  between operations: 13.4 us -> 0.02 us
  other arithmetic: 9.81 us -> 0 us
    all_gather x3 -> x0, waiting for transfers between devices: 151 us -> none  [the longest x1 84.2 us: per_device(): all_query = lax.all_gather(own_query, 'ctx', axis=0, tiled=True)]
    all_gather x2 -> x0, blocking collectives: 103 us -> none  [the longest x1 73.7 us: per_device(): lax.all_gather(own_values, 'ctx', axis=0, tiled=True)]
    pallas_call x0 -> x1, Pallas kernels: none -> 69.7 us  [per_device(): pl.pallas_call(functools.partial(kernel, n), out_shape=jax.ShapeDtypeStru...]
    all_to_all x2 -> x0, blocking collectives: 36.1 us -> none  [the longest x1 22.7 us: per_device(): lax.all_to_all(output, 'head', split_axis=0, concat_axis=1, tiled=True)]
    dot_general x10 -> x0, matrix products: 24.1 us -> none  [the longest x5 14.9 us: attend(): jnp.einsum('hrk,hkd->hrd', weights.astype(jnp.bfloat16), v_heads, preferr...]
    all_to_all x5 -> x0, starting transfers between devices: 23.8 us -> none  [the longest x1 7.75 us: per_device(): lax.all_to_all(continuation_values[0], 'head', split_axis=1, concat_axis=...]
    all_to_all x5 -> x0, waiting for transfers between devices: 12.4 us -> none  [the longest x1 7.77 us: per_device(): lax.all_to_all(top_t, 'ctx', split_axis=0, concat_axis=0, tiled=True)]
    transpose x8 -> x0, local copies, waits for them, and re-layouts: 8.06 us -> none  [the longest x3 6.27 us: split_heads(): return jnp.transpose(shaped, (1, 0, 2, 3)).reshape(kv_heads, -1, HEAD_SIZE)]
  transfers between devices with their start and end apart: 8 -> 0, of which waited for: 5 -> 0; matrix products, arithmetic and copies ran while one was open for 13% -> 0% of each run, Pallas kernels for 0% -> 0%
where the time goes in v1:
time: 76.5 us; the launch traced here: 75 us
  Pallas kernels  69.7 us (91%)
  local copies, waits for them, and re-layouts  5.33 us (7%)
    pallas_call x1, Pallas kernels, per_device(): pl.pallas_call(functools.partial(kernel, n), out_shape=jax.ShapeDtypeStru...  69.7 us
    unnamed x13, local copies, waits for them, and re-layouts  5.33 us

profile of v1, /device:TPU:1, one launch (start us, length us, event | category | flops | bytes accessed | tf_op | source)
XLA Modules:
  0.0 75.0 jit_solution(8099473431370430262)
XLA Ops:
  0.0 0.0 copy-start
  0.0 0.9 %copy-done = bf16[256,256]{1,0:T(8,128)(2,1)S(1)} copy-done((bf16[256,256]{1,0:T(8,128)(2,1)S(1)}, bf16[256,256]{1,0:T(8,128)(2,1)}, u32[]{:S(2)}) %copy-start) | copy-done | bytes 131096
  0.9 0.0 copy-start.1
  0.9 0.9 %copy-done.1 = bf16[256,256]{1,0:T(8,128)(2,1)S(1)} copy-done((bf16[256,256]{1,0:T(8,128)(2,1)S(1)}, bf16[256,256]{1,0:T(8,128)(2,1)}, u32[]{:S(2)}) %copy-start.1) | copy-done | bytes 131096
  1.8 0.0 copy-start.2
  1.8 0.8 %copy-done.2 = bf16[1,4,8192]{2,1,0:T(4,128)(2,1)S(1)} copy-done((bf16[1,4,8192]{2,1,0:T(4,128)(2,1)S(1)}, bf16[1,4,8192]{2,1,0:T(4,128)(2,1)}, u32[]{:S(2)}) %copy-start.2) | copy-done | bytes 65560
  2.6 0.0 copy-start.3
  2.7 0.7 copy-done.3
  3.3 0.0 copy-start.4
  3.3 0.7 copy-done.4
  4.0 0.0 copy-start.5
  4.0 0.7 copy-done.5
  4.7 69.7 %shard_map.64 = bf16[8,32,128]{2,1,0:T(8,128)(2,1)S(1)} custom-call(bf16[1,4,8192]{2,1,0:T(4,128)(2,1)S(1)} %copy-done.2, bf16[1,4,1024]{2,1,0:T(4,128)(2,1)S(1)} %copy-done.3, bf16[1,4,1024]{2,1,0:T(4,128)(2,1)S(1)} %copy-done.4, s32[1,8]{1,0:T(1,128)S(1)} %copy-done.5, bf16[256,256]{1,0:T(8,128)(2,1)S(1)} %copy-done, bf16[256,256]{1,0:T(8,128)(2,1)S(1)} %copy-done.1), custom_call_target="tpu_custom_call" | custom-call | flops 4300000256 | bytes 1000000 | tf_op jit(solution)/shard_map/pallas_call | solution.py:380
  74.4 0.6 copy.9
Async XLA Ops:
  0.0 0.9 %copy-start = (bf16[256,256]{1,0:T(8,128)(2,1)S(1)}, bf16[256,256]{1,0:T(8,128)(2,1)}, u32[]{:S(2)}) copy-start(bf16[256,256]{1,0:T(8,128)(2,1)} %pk_ref.1) | copy-start | bytes 393220
  0.9 0.9 %copy-start.1 = (bf16[256,256]{1,0:T(8,128)(2,1)S(1)}, bf16[256,256]{1,0:T(8,128)(2,1)}, u32[]{:S(2)}) copy-start(bf16[256,256]{1,0:T(8,128)(2,1)} %pv_ref.1) | copy-start | bytes 393220
  1.8 0.8 %copy-start.2 = (bf16[1,4,8192]{2,1,0:T(4,128)(2,1)S(1)}, bf16[1,4,8192]{2,1,0:T(4,128)(2,1)}, u32[]{:S(2)}) copy-start(bf16[1,4,8192]{2,1,0:T(4,128)(2,1)} %q_ref.1) | copy-start | bytes 196612
  2.6 0.7 copy-start.3
  3.3 0.7 copy-start.4
  4.0 0.7 copy-start.5

commit v2 on v1

v2 whole, which is shorter than its diff:
```python
import functools
import math

import jax
import jax.numpy as jnp
from jax import lax
from jax.experimental import pallas as pl
from jax.experimental.pallas import tpu as pltpu
from jax.sharding import PartitionSpec as P

MESH = pl.DeviceIdType.MESH
BF = jnp.bfloat16
F32 = jnp.float32
HEAD_SIZE = 128
SCALE = HEAD_SIZE ** -0.5
EXP2_SCALE = SCALE * math.log2(math.e)
TILE = 256
CHUNK = TILE + 64
MASKED = -1e30


def dot_nt(a, b):
    return lax.dot_general(a, b, (((1,), (1,)), ((), ())), preferred_element_type=F32)


def lanes(parts):
    return [p[:, i : i + 128] for p in parts for i in range(0, p.shape[1], 128)]


def fold(op, parts):
    parts = list(parts)
    while len(parts) > 1:
        pairs = [op(a, b) for a, b in zip(parts[::2], parts[1::2])]
        parts = pairs + (parts[-1:] if len(parts) % 2 else [])
    return parts[0]


def advance(state, scores, values):
    top = jnp.max(fold(jnp.maximum, lanes(scores)), axis=1, keepdims=True)
    if state is None:
        top = jnp.broadcast_to(top, (top.shape[0], 128))
    else:
        old = state[0]
        top = jnp.maximum(old, top)
        fade = jnp.exp2((old - top) * EXP2_SCALE)
    weights = [
        [jnp.exp2((s - top) * EXP2_SCALE) for s in lanes([part])] for part in scores
    ]
    total = fold(jnp.add, [w for part in weights for w in part])
    mixed = fold(
        jnp.add,
        [
            jnp.dot(jnp.concatenate([w.astype(BF) for w in part], axis=1), v, preferred_element_type=F32)
            for part, v in zip(weights, values)
        ],
    )
    if state is not None:
        total = total + fade * state[1]
        mixed = mixed + fade * state[2]
    return top, total, mixed


def right_slot(s):
    return 2 * s - 1 if s else 0


def left_slot(n, s):
    return 2 * s if s < n // 2 else n - 1


ORDER = ("10", "11", "X0", "X1", "S", "20", "21", "12", "13", "N",)
UNITS = {0: ("22", "23",), 1: ("30", "31",), 2: ("32", "33",), 3: ("F",), 5: ("40", "41", "42", "43",)}
FIRST = 3


def kernel(
    n, q_hbm, ck_hbm, cv_hbm, len_hbm, pk_ref, pv_ref, out_ref,
    ck_ref, cv_ref, len_ref,
    stage, outbox, inbox, kvb, others, qb, top, total, mixed, ckb, cvb,
    osend, lsend, orecv, lrecv, fsend, frecv,
    own_sem, box_send, box_recv, pair_send, pair_recv, kv_send, kv_recv,
    q_send, q_recv, o_send, o_recv, l_send, l_recv, f_send, f_recv,
):
    half, near = n // 2, n // 4
    ctx, z, head = lax.axis_index("ctx"), lax.axis_index("cand"), lax.axis_index("head")
    y, xh, core = ctx // 2, ctx % 2, head % 2
    me = xh * 4 + head
    kv_head = 2 * head + xh

    def around(a, s):
        return lax.rem(a + s + n, n)

    u = z + core * (y - z)
    v = y + core * (around(z, -half) - y)

    def device(uu, vv):
        return ((vv + core * (uu - vv)) * 2 + xh, uu + core * (around(vv, half) - uu), head)

    members = [(e // 4, e % 4) for e in range(8)]
    here = core == 0

    def source(e):
        return (v * 2 + members[e][0], u, members[e][1])

    def target(e):
        return (y * 2 + members[e][0], z, members[e][1]) if e % 2 == 0 else (z * 2 + members[e][0], around(y, half), members[e][1])

    def other(e):
        return jnp.logical_not((me == e) & here)

    loads = [
        pltpu.make_async_copy(src, dst, own_sem.at[2 + i])
        for i, (src, dst) in enumerate(((q_hbm, outbox.at[:, 0:32]), (ck_hbm, ck_ref), (cv_hbm, cv_ref), (len_hbm, len_ref)))
    ]
    own_copies = [
        pltpu.make_async_copy(
            ref.at[:, pl.ds(pl.multiple_of(at * 128, 128), 128)], dst.at[i], own_sem.at[sem + i]
        )
        for at, dst, sem in ((xh, kvb.at[0, 0], 0), (1 - xh, others, 6))
        for i, ref in enumerate((pk_ref, pv_ref))
    ]
    for c in loads + own_copies:
        c.start()

    barrier = pltpu.get_barrier_semaphore()

    def greet(to):
        pl.semaphore_signal(barrier, inc=1, device_id=to, device_id_type=MESH)

    for e in range(8):
        @pl.when(other(e))
        def _():
            greet(source(e))
            greet(target(e))
    partner = (y * 2 + 1 - xh, z, head)
    greet(partner)
    for s in range(1, n):
        greet(device(u, around(v, s)))
    right, left = device(around(u, 1), v), device(around(u, -1), v)
    greet(right)
    greet(left)

    for c in loads:
        c.wait()
    ends, so_far = [], 0
    for c in range(8):
        so_far = so_far + len_ref[0, c]
        ends.append(so_far)
    place = lax.broadcasted_iota(jnp.int32, (8, 128), 1) + 128 * lax.broadcasted_iota(jnp.int32, (8, 128), 0)
    segment = fold(jnp.add, [jnp.where(end <= place, 1.0, 0.0) for end in ends])
    cks, cvs = ck_ref[...].astype(F32), cv_ref[...].astype(F32)
    for k in range(8):
        stage[0:4] = cks[k * 4 : k * 4 + 4]
        stage[4:8] = cvs[k * 4 : k * 4 + 4]
        stage[8:16] = segment
        outbox[k, 32:48, :] = stage[0:16].astype(BF)

    pl.semaphore_wait(barrier, 1 + (n - 1) + 2 + 16 - 2 * here.astype(jnp.int32))

    def remote(src, dst, send, recv, to):
        return pltpu.make_async_remote_copy(
            src_ref=src, dst_ref=dst, send_sem=send, recv_sem=recv, device_id=to, device_id_type=MESH
        )

    def box(e):
        k = 2 * members[e][1] + members[e][0]
        return remote(outbox.at[k], inbox.at[me], box_send.at[e], box_recv.at[me], target(e))

    def box_in(e):
        return remote(outbox.at[0], inbox.at[e], box_send.at[e], box_recv.at[e], source(e))

    for e in range(8):
        @pl.when(other(e))
        def _():
            box(e).start()

        @pl.when(jnp.logical_not(other(e)))
        def _():
            inbox[e] = outbox[kv_head]
    crossing = [remote(others.at[i], kvb.at[0, 1, i], pair_send.at[i], pair_recv.at[i], partner) for i in (0, 1)]

    def kv_copies(s, piece):
        out = []
        sub, i = piece // 2, piece % 2
        for sign, slot, to in ((1, right_slot, right), (-1, functools.partial(left_slot, n), left)):
            if s == half and sub == (sign > 0):
                continue
            src, dst = slot(s - 1) if s > 1 else 0, slot(s)
            out.append(remote(kvb.at[src, sub, i], kvb.at[dst, sub, i], kv_send.at[dst, piece], kv_recv.at[dst, piece], to))
        return out

    def kv_do(s, piece, act):
        if s <= half:
            for c in kv_copies(s, piece):
                act(c)

    def kv_event(s, piece):
        kv_do(s, piece, lambda c: c.wait_recv())
        if s < half:
            kv_do(s + 1, piece, lambda c: c.start())

    for c in own_copies[2:]:
        c.wait()
    for c in crossing:
        c.start()

    for i in (0, 1):
        own_copies[i].wait()
        kv_do(1, i, lambda c: c.start())

    def q_copies(far):
        out = []
        for s in range(1, near + 1):
            for sign, slot in ((1, right_slot), (-1, functools.partial(left_slot, n))):
                src, dst = (slot(near), slot(near + s)) if far else (0, slot(s))
                last = near + s == half
                rows = pl.ds(0, CHUNK)
                if far and last:
                    rows = pl.ds(0 if sign > 0 else CHUNK // 2, CHUNK // 2)
                sem = n if far and last and sign < 0 else dst
                out.append(remote(
                    qb.at[src, rows], qb.at[dst, rows], q_send.at[sem], q_recv.at[sem], device(u, around(v, sign * s))
                ))
        return out

    def q_do(far, act):
        for c in q_copies(far):
            act(c)

    def scattered():
        for e in range(8):
            @pl.when(other(e))
            def _():
                box_in(e).wait_recv()
        for e in range(8):
            qb[0, e * 32 : e * 32 + 32, :] = inbox[e, 0:32, :]
            extra = inbox[e, 32:48, :].astype(F32)
            stage[e * 4 : e * 4 + 4] = extra[0:4]
            stage[32 + e * 4 : 32 + e * 4 + 4] = extra[4:8]
        qb[0, TILE : TILE + 64, :] = stage[...].astype(BF)
        q_do(False, lambda c: c.start())

    def run(order):
        for token in order:
            if token == "S":
                scattered()
            elif token == "N":
                q_do(False, lambda c: c.wait_recv())
                q_do(True, lambda c: c.start())
            elif token == "F":
                q_do(True, lambda c: c.wait_recv())
            elif token[0] == "X":
                i = int(token[1])
                crossing[i].wait_recv()
                kv_do(1, 2 + i, lambda c: c.start())
            else:
                kv_event(int(token[0]), int(token[1]))

    run(ORDER)

    def own_continuation():
        for r in range(n):
            d = -((r + 1) // 2) if r % 2 else r // 2
            at = pl.ds(pl.multiple_of(around(v, d) * 32, 32), 32)
            ckb[at, :] = qb[r, TILE : TILE + 32, :]
            cvb[at, :] = qb[r, TILE + 32 : TILE + 64, :]
        wide = min(128, 32 * n)
        marks = inbox[0, 32:48, :].astype(F32)
        row = lax.broadcasted_iota(jnp.int32, (TILE, wide), 0)
        slot = v * 32 + (row // 32) * 4 + row % 4
        lane = lax.broadcasted_iota(jnp.int32, (TILE, wide), 1)
        halves = range(32 * n // wide)
        own = fold(jnp.add, [
            jnp.sum(jnp.where(lane + h * wide == slot, marks[8 + h : 9 + h, :wide], 0.0), axis=1, keepdims=True) for h in halves
        ])
        scores = []
        for h in halves:
            allowed = (marks[8 + h : 9 + h, :wide] == own) & (lane + h * wide <= slot)
            scores.append(jnp.where(allowed, dot_nt(qb[0, 0:TILE, :], ckb[h * wide : (h + 1) * wide, :]), MASKED))
        state = (top[0], total[0], mixed[0])
        top[0], total[0], mixed[0] = advance(state, scores, [cvb[h * wide : (h + 1) * wide, :] for h in halves])

    row = lax.broadcasted_iota(jnp.int32, (128, 128), 0)
    lane = lax.broadcasted_iota(jnp.int32, (128, 128), 1)
    diagonal = row == lane

    def finish(r):
        w = jnp.sum(total[r], axis=1, keepdims=True)
        lse = top[r] * SCALE + jnp.log(w)
        for h in range(2):
            lsend[r, h : h + 1, :] = jnp.sum(
                jnp.where(diagonal, lse[h * 128 : h * 128 + 128], 0.0), axis=0, keepdims=True
            )
        return mixed[r] / w

    def o_copies(r):
        odd = r % 2
        mirror = r + 2 * odd - 1 - r // (n - 1)
        to = device(u, around(v, (1 - odd) * (r // 2) - odd * ((r + 1) // 2)))
        return [
            remote(osend.at[r], orecv.at[mirror], o_send.at[r], o_recv.at[mirror], to),
            remote(lsend.at[r], lrecv.at[mirror], l_send.at[r], l_recv.at[mirror], to),
        ]

    def give(r, _):
        osend[r] = finish(r).astype(BF)
        for c in o_copies(r):
            c.start()
        return 0

    def each_sent(act):
        def one(r, _):
            for c in o_copies(r):
                act(c)
            return 0

        lax.fori_loop(1, n, one, 0)

    pairs, tiles = n // 2, n // 2
    first = FIRST if n == 8 else 1
    before = UNITS if n == 8 else {1: ("F",)}
    top[...] = jnp.full(top.shape, MASKED, F32)
    total[...] = jnp.zeros(total.shape, F32)
    mixed[...] = jnp.zeros(mixed.shape, F32)

    def visit(i, _):
        for at, events in before.items():
            @pl.when(i == at)
            def _():
                run(events)

        second, third = (i + 2 * pairs - first) // (2 * pairs), (i + pairs - first) // (2 * pairs)
        part, p = second - third, i - first * second - (pairs - first) * third
        rows = pl.ds(part * tiles, tiles)
        q = jnp.concatenate([qb[part * tiles + r, 0:TILE, :] for r in range(tiles)], axis=0)
        pieces = [(2 * p + s, ab) for s in (0, 1) for ab in (0, 1)]
        scores = [dot_nt(q, kvb[s, ab, 0]) for s, ab in pieces]
        state = tuple(x[rows].reshape(tiles * TILE, 128) for x in (top, total, mixed))
        state = advance(state, scores, [kvb[s, ab, 1] for s, ab in pieces])
        for x, new in zip((top, total, mixed), state):
            x[rows] = new.reshape(tiles, TILE, 128)

        @pl.when(i == first + pairs - 1)
        def _():
            lax.fori_loop(tiles, n, give, 0)
            own_continuation()

        return 0

    lax.fori_loop(0, 2 * pairs, visit, 0)

    lax.fori_loop(1, tiles, give, 0)
    mine = finish(0)
    each_sent(lambda c: c.wait_recv())
    pieces = [lsend[0, 0:2, :]] + [lrecv[r, 0:2, :] for r in range(1, n)]
    largest = fold(jnp.maximum, pieces)
    shares = [jnp.exp(p - largest) for p in pieces]
    whole = fold(jnp.add, shares)
    shares = [p / whole for p in shares]
    for h in range(2):
        rows = slice(h * 128, h * 128 + 128)
        terms = []
        for r in range(n):
            share = jnp.sum(jnp.where(diagonal, shares[r][h : h + 1, :], 0.0), axis=1, keepdims=True)
            terms.append(share * (mine[rows] if r == 0 else orecv[r, rows, :].astype(F32)))
        fsend[rows, :] = fold(jnp.add, terms).astype(BF)

    def final(e):
        return remote(fsend.at[e * 32 : e * 32 + 32], frecv.at[kv_head], f_send.at[e], f_recv.at[kv_head], source(e))

    def final_in(e):
        k = 2 * members[e][1] + members[e][0]
        return remote(fsend.at[0:32], frecv.at[k], f_send.at[e], f_recv.at[k], target(e))

    for e in range(8):
        @pl.when(other(e))
        def _():
            final(e).start()

        @pl.when(jnp.logical_not(other(e)))
        def _():
            frecv[kv_head] = fsend[e * 32 : e * 32 + 32, :]

    each_sent(lambda c: c.wait_send())
    for c in crossing:
        c.wait_send()
    for s in range(1, half + 1):
        for piece in range(4):
            kv_do(s, piece, lambda c: c.wait_send())
    q_do(False, lambda c: c.wait_send())
    q_do(True, lambda c: c.wait_send())
    for e in range(8):
        @pl.when(other(e))
        def _():
            box(e).wait_send()
            final(e).wait_send()
            final_in(e).wait_recv()
    out_ref[...] = frecv[...]


def by_head(flat, heads):
    return jnp.transpose(flat.reshape(4, 8 * heads, 128), (1, 0, 2)).reshape(-1, 128)


def per_device(n, query, prefix_keys, prefix_value_cache, cont_keys, continuation_values, cont_lengths):
    rows = prefix_keys.shape[0]
    vmem = pl.BlockSpec(memory_space=pltpu.VMEM)
    anywhere = pl.BlockSpec(memory_space=pltpu.MemorySpace.HBM)
    dma = pltpu.SemaphoreType.DMA
    out = pl.pallas_call(
        functools.partial(kernel, n),
        out_shape=jax.ShapeDtypeStruct((8, 32, 128), BF),
        in_specs=[anywhere] * 6,
        out_specs=vmem,
        scratch_shapes=[
            pltpu.VMEM((32, 128), BF),
            pltpu.VMEM((32, 128), BF),
            pltpu.SMEM(cont_lengths.shape, jnp.int32),
            pltpu.VMEM((64, 128), F32),
            pltpu.VMEM((8, 48, 128), BF),
            pltpu.VMEM((8, 48, 128), BF),
            pltpu.VMEM((n, 2, 2, rows, 128), BF),
            pltpu.VMEM((2, rows, 128), BF),
            pltpu.VMEM((n, CHUNK, 128), BF),
            pltpu.VMEM((n, TILE, 128), F32),
            pltpu.VMEM((n, TILE, 128), F32),
            pltpu.VMEM((n, TILE, 128), F32),
            pltpu.VMEM((32 * n, 128), BF),
            pltpu.VMEM((32 * n, 128), BF),
            pltpu.VMEM((n, TILE, 128), BF),
            pltpu.VMEM((n, 8, 128), F32),
            pltpu.VMEM((n, TILE, 128), BF),
            pltpu.VMEM((n, 8, 128), F32),
            pltpu.VMEM((TILE, 128), BF),
            pltpu.VMEM((8, 32, 128), BF),
            dma((8,)), dma((8,)), dma((8,)), dma((2,)), dma((2,)), dma((n, 4)), dma((n, 4)),
            dma((n + 1,)), dma((n + 1,)), dma((n,)), dma((n,)), dma((n,)), dma((n,)), dma((8,)), dma((8,)),
        ],
        compiler_params=pltpu.CompilerParams(
            collective_id=0, has_side_effects=True, vmem_limit_bytes=56 * 1024 * 1024
        ),
        cost_estimate=pl.CostEstimate(flops=4_300_000_000, bytes_accessed=1_000_000, transcendentals=8_400_000),
    )(*[
        pltpu.with_memory_space_constraint(x, pltpu.MemorySpace.HBM)
        for x in (
            by_head(query, 8).reshape(8, 32, 128), by_head(cont_keys, 1), by_head(continuation_values, 1),
            cont_lengths, prefix_keys, prefix_value_cache,
        )
    ])
    return jnp.transpose(out.reshape(8, 8, 4, 128), (2, 0, 1, 3)).reshape(query.shape)


def solution(mesh):
    n = mesh.shape["cand"]
    return jax.shard_map(
        functools.partial(per_device, n),
        mesh=mesh,
        in_specs=(
            P("cand", ("ctx", "head"), None),
            P(("ctx", "cand"), "head"),
            P(("ctx", "cand"), "head"),
            P("cand", ("ctx", "head"), None),
            P("cand", ("ctx", "head"), None),
            P("cand", None),
        ),
        out_specs=P("cand", ("ctx", "head"), None),
        check_vma=False,
    )
```

time: 76.5 us -> 62.7 us (0.82); the launches traced: 75 us -> 62.5 us
  Pallas kernels: 69.7 us -> 61 us
  local copies, waits for them, and re-layouts: 5.33 us -> 1.49 us
    pallas_call x1, Pallas kernels: 69.7 us -> 61 us  [per_device(): pl.pallas_call(functools.partial(kernel, n), out_shape=jax.ShapeDtypeStru...]
    unnamed x13 -> x1, local copies, waits for them, and re-layouts: 5.33 us -> 1.49 us
where the time goes in v2:
time: 62.7 us; the launch traced here: 62.5 us
  Pallas kernels  61 us (97%)
  local copies, waits for them, and re-layouts  1.49 us (2%)
    pallas_call x1, Pallas kernels, per_device(): pl.pallas_call(functools.partial(kernel, n), out_shape=jax.ShapeDtypeStru...  61 us
    unnamed x1, local copies, waits for them, and re-layouts  1.49 us

profile of v2, /device:TPU:1, one launch (start us, length us, event | category | flops | bytes accessed | tf_op | source)
XLA Modules:
  0.0 62.5 jit_solution(924486842575521207)
XLA Ops:
  0.0 61.0 %shard_map.64 = bf16[8,32,128]{2,1,0:T(8,128)(2,1)} custom-call(bf16[8,32,128]{2,1,0:T(8,128)(2,1)} %bitcast.21, bf16[32,128]{1,0:T(8,128)(2,1)} %bitcast.22, bf16[32,128]{1,0:T(8,128)(2,1)} %bitcast.23, s32[1,8]{1,0:T(1,128)} %len_hbm.1, bf16[256,256]{1,0:T(8,128)(2,1)} %pk_ref.1, bf16[256,256]{1,0:T(8,128)(2,1)} %pv_ref.1), custom_call_target="tpu_custom_call" | custom-call | flops 4300000256 | bytes 1000000 | tf_op jit(solution)/shard_map/pallas_call | solution.py:410
  61.0 1.5 %copy.12 = bf16[1,4,8192]{2,1,0:T(4,128)(2,1)} copy(bf16[1,4,8192]{2,1,0:T(4,128)(2,1)} %bitcast.20) | data formatting | bytes 131072

commit v3 on v2

--- a/solution.py
+++ b/solution.py
@@ -68,9 +68,10 @@
     return 2 * s if s < n // 2 else n - 1
 
 
-ORDER = ("10", "11", "X0", "X1", "S", "20", "21", "12", "13", "N",)
-UNITS = {0: ("22", "23",), 1: ("30", "31",), 2: ("32", "33",), 3: ("F",), 5: ("40", "41", "42", "43",)}
-FIRST = 3
+ORDER = ("S", "10", "11", "X0", "X1", "N", "20", "21", "12", "13",)
+UNITS = {1: ("30", "31",)}
+FIRST = 2
+FAR_UNITS = {2: ("22", "23", "40", "41",)}
 
 
 def kernel(
@@ -139,6 +140,9 @@
     right, left = device(around(u, 1), v), device(around(u, -1), v)
     greet(right)
     greet(left)
+    for s in range(2, near + 1):
+        greet(device(around(u, s), v))
+        greet(device(around(u, -s), v))
 
     for c in loads:
         c.wait()
@@ -155,7 +159,7 @@
         stage[8:16] = segment
         outbox[k, 32:48, :] = stage[0:16].astype(BF)
 
-    pl.semaphore_wait(barrier, 1 + (n - 1) + 2 + 16 - 2 * here.astype(jnp.int32))
+    pl.semaphore_wait(barrier, 1 + (n - 1) + 2 * near + 16 - 2 * here.astype(jnp.int32))
 
     def remote(src, dst, send, recv, to):
         return pltpu.make_async_remote_copy(
@@ -183,21 +187,29 @@
         out = []
         sub, i = piece // 2, piece % 2
         for sign, slot, to in ((1, right_slot, right), (-1, functools.partial(left_slot, n), left)):
-            if s == half and sub == (sign > 0):
-                continue
-            src, dst = slot(s - 1) if s > 1 else 0, slot(s)
-            out.append(remote(kvb.at[src, sub, i], kvb.at[dst, sub, i], kv_send.at[dst, piece], kv_recv.at[dst, piece], to))
+            if sub == 0:
+                hops = [(s - 1, s, 1)]
+            elif s == 1:
+                hops = [(0, d, d) for d in range(near, 0, -1)]
+            else:
+                hops = [(near, near + d, d) for d in range(near, 0, -1)]
+            for old, new, far in hops:
+                if new == half and sub == (sign > 0):
+                    continue
+                src, dst = slot(old) if old else 0, slot(new)
+                out.append(remote(
+                    kvb.at[src, sub, i], kvb.at[dst, sub, i], kv_send.at[dst, piece], kv_recv.at[dst, piece], device(around(u, sign * far), v)
+                ))
         return out
 
     def kv_do(s, piece, act):
-        if s <= half:
+        if s <= (half if piece < 2 else 2):
             for c in kv_copies(s, piece):
                 act(c)
 
     def kv_event(s, piece):
         kv_do(s, piece, lambda c: c.wait_recv())
-        if s < half:
-            kv_do(s + 1, piece, lambda c: c.start())
+        kv_do(s + 1, piece, lambda c: c.start())
 
     for c in own_copies[2:]:
         c.wait()
@@ -291,7 +303,7 @@
             lsend[r, h : h + 1, :] = jnp.sum(
                 jnp.where(diagonal, lse[h * 128 : h * 128 + 128], 0.0), axis=0, keepdims=True
             )
-        return mixed[r] / w
+        return mixed[r] * (1.0 / w)
 
     def o_copies(r):
         odd = r % 2
@@ -316,40 +328,72 @@
 
         lax.fori_loop(1, n, one, 0)
 
-    pairs, tiles = n // 2, n // 2
-    first = FIRST if n == 8 else 1
-    before = UNITS if n == 8 else {1: ("F",)}
+    pairs, tiles = n // 2, 2 * near + 1
+    first = min(FIRST, pairs)
+    before = UNITS if n == 8 else {0: ("22", "23")}
     top[...] = jnp.full(top.shape, MASKED, F32)
     total[...] = jnp.zeros(total.shape, F32)
     mixed[...] = jnp.zeros(mixed.shape, F32)
 
-    def visit(i, _):
+    def unit(low, count, p):
+        rows = pl.ds(low, count)
+        q = jnp.concatenate([qb[low + r, 0:TILE, :] for r in range(count)], axis=0)
+        pieces = [(2 * p + s, ab) for s in (0, 1) for ab in (0, 1)]
+        scores = [dot_nt(q, kvb[s, ab, 0]) for s, ab in pieces]
+        state = tuple(x[rows].reshape(count * TILE, 128) for x in (top, total, mixed))
+        state = advance(state, scores, [kvb[s, ab, 1] for s, ab in pieces])
+        for x, new in zip((top, total, mixed), state):
+            x[rows] = new.reshape(count, TILE, 128)
+
+    def near_unit(p, _):
         for at, events in before.items():
-            @pl.when(i == at)
+            @pl.when(p == at)
             def _():
                 run(events)
 
-        second, third = (i + 2 * pairs - first) // (2 * pairs), (i + pairs - first) // (2 * pairs)
-        part, p = second - third, i - first * second - (pairs - first) * third
-        rows = pl.ds(part * tiles, tiles)
-        q = jnp.concatenate([qb[part * tiles + r, 0:TILE, :] for r in range(tiles)], axis=0)
-        pieces = [(2 * p + s, ab) for s in (0, 1) for ab in (0, 1)]
-        scores = [dot_nt(q, kvb[s, ab, 0]) for s, ab in pieces]
-        state = tuple(x[rows].reshape(tiles * TILE, 128) for x in (top, total, mixed))
-        state = advance(state, scores, [kvb[s, ab, 1] for s, ab in pieces])
-        for x, new in zip((top, total, mixed), state):
-            x[rows] = new.reshape(tiles, TILE, 128)
-
-        @pl.when(i == first + pairs - 1)
-        def _():
-            lax.fori_loop(tiles, n, give, 0)
-            own_continuation()
-
+        unit(0, tiles, p)
         return 0
 
-    lax.fori_loop(0, 2 * pairs, visit, 0)
-
-    lax.fori_loop(1, tiles, give, 0)
+    def far_unit(p, _):
+        for at, events in FAR_UNITS.items() if n == 8 else ():
+            @pl.when(p == at)
+            def _():
+                run(events)
+
+        unit(tiles, n - tiles, p)
+        return 0
+
+    def give_all(low, high):
+        lax.fori_loop(0, high - low, lambda i, c: give(high - 1 - i, c), 0)
+
+    lax.fori_loop(0, first, near_unit, 0)
+    if first == pairs:
+        give_all(1, tiles)
+    run(("F",))
+    lax.fori_loop(0, pairs, far_unit, 0)
+    give_all(tiles, n)
+    if first < pairs:
+        lax.fori_loop(first, pairs, near_unit, 0)
+        give_all(1, tiles)
+    own_continuation()
+
+    def final(e):
+        return remote(fsend.at[e * 32 : e * 32 + 32], frecv.at[kv_head], f_send.at[e], f_recv.at[kv_head], source(e))
+
+    def final_in(e):
+        k = 2 * members[e][1] + members[e][0]
+        return remote(fsend.at[0:32], frecv.at[k], f_send.at[e], f_recv.at[k], target(e))
+
+    def send_back(some):
+        for e in some:
+            @pl.when(other(e))
+            def _():
+                final(e).start()
+
+            @pl.when(jnp.logical_not(other(e)))
+            def _():
+                frecv[kv_head] = fsend[e * 32 : e * 32 + 32, :]
+
     mine = finish(0)
     each_sent(lambda c: c.wait_recv())
     pieces = [lsend[0, 0:2, :]] + [lrecv[r, 0:2, :] for r in range(1, n)]
@@ -364,22 +408,7 @@
             share = jnp.sum(jnp.where(diagonal, shares[r][h : h + 1, :], 0.0), axis=1, keepdims=True)
             terms.append(share * (mine[rows] if r == 0 else orecv[r, rows, :].astype(F32)))
         fsend[rows, :] = fold(jnp.add, terms).astype(BF)
-
-    def final(e):
-        return remote(fsend.at[e * 32 : e * 32 + 32], frecv.at[kv_head], f_send.at[e], f_recv.at[kv_head], source(e))
-
-    def final_in(e):
-        k = 2 * members[e][1] + members[e][0]
-        return remote(fsend.at[0:32], frecv.at[k], f_send.at[e], f_recv.at[k], target(e))
-
-    for e in range(8):
-        @pl.when(other(e))
-        def _():
-            final(e).start()
-
-        @pl.when(jnp.logical_not(other(e)))
-        def _():
-            frecv[kv_head] = fsend[e * 32 : e * 32 + 32, :]
+        send_back(range(h * 4, h * 4 + 4))
 
     each_sent(lambda c: c.wait_send())
     for c in crossing:
@@ -437,7 +466,7 @@
             dma((n + 1,)), dma((n + 1,)), dma((n,)), dma((n,)), dma((n,)), dma((n,)), dma((8,)), dma((8,)),
         ],
         compiler_params=pltpu.CompilerParams(
-            collective_id=0, has_side_effects=True, vmem_limit_bytes=56 * 1024 * 1024
+            collective_id=0, has_side_effects=True, vmem_limit_bytes=40 * 1024 * 1024
         ),
         cost_estimate=pl.CostEstimate(flops=4_300_000_000, bytes_accessed=1_000_000, transcendentals=8_400_000),
     )(*[

time: 62.7 us -> 59.2 us (0.944)
  Pallas kernels: 61 us -> 58.4 us
  local copies, waits for them, and re-layouts: 1.49 us -> 0.63 us
    pallas_call x1, Pallas kernels: 61 us -> 58.4 us  [per_device(): pl.pallas_call(functools.partial(kernel, n), out_shape=jax.ShapeDtypeStru...]
    unnamed x1, local copies, waits for them, and re-layouts: 1.49 us -> 0.63 us
where the time goes in v3:
time: 59.2 us; the launch traced here: 59.1 us
  Pallas kernels  58.4 us (99%)
  local copies, waits for them, and re-layouts  0.63 us (1%)
    pallas_call x1, Pallas kernels, per_device(): pl.pallas_call(functools.partial(kernel, n), out_shape=jax.ShapeDtypeStru...  58.4 us

profile of v3, /device:TPU:1, one launch (start us, length us, event | category | flops | bytes accessed | tf_op | source)
XLA Modules:
  0.0 59.1 jit_solution(1097193476246391694)
XLA Ops:
  0.0 58.4 %shard_map.64 = bf16[8,32,128]{2,1,0:T(8,128)(2,1)S(1)} custom-call(bf16[8,32,128]{2,1,0:T(8,128)(2,1)} %bitcast.21, bf16[32,128]{1,0:T(8,128)(2,1)} %bitcast.22, bf16[32,128]{1,0:T(8,128)(2,1)} %bitcast.23, s32[1,8]{1,0:T(1,128)} %len_hbm.1, bf16[256,256]{1,0:T(8,128)(2,1)} %pk_ref.1, bf16[256,256]{1,0:T(8,128)(2,1)} %pv_ref.1), custom_call_target="tpu_custom_call" | custom-call | flops 4300000256 | bytes 1000000 | tf_op jit(solution)/shard_map/pallas_call | solution.py:439
  58.4 0.6 %copy.12 = bf16[1,4,8192]{2,1,0:T(4,128)(2,1)} copy(bf16[1,4,8192]{2,1,0:T(4,128)(2,1)S(1)} %bitcast.20) | data formatting | bytes 131072

commit v4 on v3

--- a/solution.py
+++ b/solution.py
@@ -68,10 +68,16 @@
     return 2 * s if s < n // 2 else n - 1
 
 
+def place_of(n, slot, sub):
+    if slot in (0, n - 1):
+        return 2 * slot + sub
+    return 4 * ((slot + 1) // 2) - 2 + 2 * sub + (slot + 1) % 2
+
+
 ORDER = ("S", "10", "11", "X0", "X1", "N", "20", "21", "12", "13",)
 UNITS = {1: ("30", "31",)}
 FIRST = 2
-FAR_UNITS = {2: ("22", "23", "40", "41",)}
+FAR_UNITS = {3: ("22", "23", "40", "41",)}
 
 
 def kernel(
@@ -117,7 +123,7 @@
         pltpu.make_async_copy(
             ref.at[:, pl.ds(pl.multiple_of(at * 128, 128), 128)], dst.at[i], own_sem.at[sem + i]
         )
-        for at, dst, sem in ((xh, kvb.at[0, 0], 0), (1 - xh, others, 6))
+        for at, dst, sem in ((xh, kvb.at[0], 0), (1 - xh, others, 6))
         for i, ref in enumerate((pk_ref, pv_ref))
     ]
     for c in loads + own_copies:
@@ -132,11 +138,11 @@
         @pl.when(other(e))
         def _():
             greet(source(e))
-            greet(target(e))
     partner = (y * 2 + 1 - xh, z, head)
     greet(partner)
-    for s in range(1, n):
+    for s in range(1, near + 1):
         greet(device(u, around(v, s)))
+        greet(device(u, around(v, -s)))
     right, left = device(around(u, 1), v), device(around(u, -1), v)
     greet(right)
     greet(left)
@@ -159,7 +165,11 @@
         stage[8:16] = segment
         outbox[k, 32:48, :] = stage[0:16].astype(BF)
 
-    pl.semaphore_wait(barrier, 1 + (n - 1) + 2 * near + 16 - 2 * here.astype(jnp.int32))
+    top[...] = jnp.full(top.shape, MASKED, F32)
+    total[...] = jnp.zeros(total.shape, F32)
+    mixed[...] = jnp.zeros(mixed.shape, F32)
+
+    pl.semaphore_wait(barrier, 1 + 4 * near + 8 - here.astype(jnp.int32))
 
     def remote(src, dst, send, recv, to):
         return pltpu.make_async_remote_copy(
@@ -181,7 +191,7 @@
         @pl.when(jnp.logical_not(other(e)))
         def _():
             inbox[e] = outbox[kv_head]
-    crossing = [remote(others.at[i], kvb.at[0, 1, i], pair_send.at[i], pair_recv.at[i], partner) for i in (0, 1)]
+    crossing = [remote(others.at[i], kvb.at[1, i], pair_send.at[i], pair_recv.at[i], partner) for i in (0, 1)]
 
     def kv_copies(s, piece):
         out = []
@@ -198,7 +208,7 @@
                     continue
                 src, dst = slot(old) if old else 0, slot(new)
                 out.append(remote(
-                    kvb.at[src, sub, i], kvb.at[dst, sub, i], kv_send.at[dst, piece], kv_recv.at[dst, piece], device(around(u, sign * far), v)
+                    kvb.at[place_of(n, src, sub), i], kvb.at[place_of(n, dst, sub), i], kv_send.at[dst, piece], kv_recv.at[dst, piece], device(around(u, sign * far), v)
                 ))
         return out
 
@@ -252,6 +262,19 @@
         qb[0, TILE : TILE + 64, :] = stage[...].astype(BF)
         q_do(False, lambda c: c.start())
 
+    def unit(low, count, p):
+        rows = pl.ds(low, count)
+        q = jnp.concatenate([qb[low + r, 0:TILE, :] for r in range(count)], axis=0)
+        scores = [dot_nt(q, kvb[4 * p + i, 0]) for i in range(4)]
+        state = tuple(x[rows].reshape(count * TILE, 128) for x in (top, total, mixed))
+        state = advance(state, scores, [kvb[4 * p + i, 1] for i in range(4)])
+        for x, new in zip((top, total, mixed), state):
+            x[rows] = new.reshape(count, TILE, 128)
+
+    def own_unit(p, _):
+        unit(0, 1, p)
+        return 0
+
     def run(order):
         for token in order:
             if token == "S":
@@ -259,6 +282,8 @@
             elif token == "N":
                 q_do(False, lambda c: c.wait_recv())
                 q_do(True, lambda c: c.start())
+            elif token == "O":
+                own_unit(0, 0)
             elif token == "F":
                 q_do(True, lambda c: c.wait_recv())
             elif token[0] == "X":
@@ -331,27 +356,13 @@
     pairs, tiles = n // 2, 2 * near + 1
     first = min(FIRST, pairs)
     before = UNITS if n == 8 else {0: ("22", "23")}
-    top[...] = jnp.full(top.shape, MASKED, F32)
-    total[...] = jnp.zeros(total.shape, F32)
-    mixed[...] = jnp.zeros(mixed.shape, F32)
-
-    def unit(low, count, p):
-        rows = pl.ds(low, count)
-        q = jnp.concatenate([qb[low + r, 0:TILE, :] for r in range(count)], axis=0)
-        pieces = [(2 * p + s, ab) for s in (0, 1) for ab in (0, 1)]
-        scores = [dot_nt(q, kvb[s, ab, 0]) for s, ab in pieces]
-        state = tuple(x[rows].reshape(count * TILE, 128) for x in (top, total, mixed))
-        state = advance(state, scores, [kvb[s, ab, 1] for s, ab in pieces])
-        for x, new in zip((top, total, mixed), state):
-            x[rows] = new.reshape(count, TILE, 128)
-
     def near_unit(p, _):
         for at, events in before.items():
             @pl.when(p == at)
             def _():
                 run(events)
 
-        unit(0, tiles, p)
+        unit(1, tiles - 1, p)
         return 0
 
     def far_unit(p, _):
@@ -375,6 +386,7 @@
     if first < pairs:
         lax.fori_loop(first, pairs, near_unit, 0)
         give_all(1, tiles)
+    lax.fori_loop(0, pairs, own_unit, 0)
     own_continuation()
 
     def final(e):
@@ -448,7 +460,7 @@
             pltpu.VMEM((64, 128), F32),
             pltpu.VMEM((8, 48, 128), BF),
             pltpu.VMEM((8, 48, 128), BF),
-            pltpu.VMEM((n, 2, 2, rows, 128), BF),
+            pltpu.VMEM((2 * n, 2, rows, 128), BF),
             pltpu.VMEM((2, rows, 128), BF),
             pltpu.VMEM((n, CHUNK, 128), BF),
             pltpu.VMEM((n, TILE, 128), F32),

time: 59.2 us -> 58.3 us (0.985)
  Pallas kernels: 58.4 us -> 57.5 us
    pallas_call x1, Pallas kernels: 58.4 us -> 57.5 us  [per_device(): pl.pallas_call(functools.partial(kernel, n), out_shape=jax.ShapeDtypeStru...]
where the time goes in v4:
time: 58.3 us; the launch traced here: 58.1 us
  Pallas kernels  57.5 us (99%)
  local copies, waits for them, and re-layouts  0.63 us (1%)
    pallas_call x1, Pallas kernels, per_device(): pl.pallas_call(functools.partial(kernel, n), out_shape=jax.ShapeDtypeStru...  57.5 us

profile of v4, /device:TPU:1, one launch (start us, length us, event | category | flops | bytes accessed | tf_op | source)
XLA Modules:
  0.0 58.1 jit_solution(6592621618433583428)
XLA Ops:
  0.0 57.5 %shard_map.64 = bf16[8,32,128]{2,1,0:T(8,128)(2,1)S(1)} custom-call(bf16[8,32,128]{2,1,0:T(8,128)(2,1)} %bitcast.21, bf16[32,128]{1,0:T(8,128)(2,1)} %bitcast.22, bf16[32,128]{1,0:T(8,128)(2,1)} %bitcast.23, s32[1,8]{1,0:T(1,128)} %len_hbm.1, bf16[256,256]{1,0:T(8,128)(2,1)} %pk_ref.1, bf16[256,256]{1,0:T(8,128)(2,1)} %pv_ref.1), custom_call_target="tpu_custom_call" | custom-call | flops 4300000256 | bytes 1000000 | tf_op jit(solution)/shard_map/pallas_call | solution.py:451
  57.5 0.6 %copy.12 = bf16[1,4,8192]{2,1,0:T(4,128)(2,1)} copy(bf16[1,4,8192]{2,1,0:T(4,128)(2,1)S(1)} %bitcast.20) | data formatting | bytes 131072
